TPU v7x, 32 devices: a whole 2x2x4 slice. The times are simulated.
32 devices in a mesh: row: 4 (over x, core), col: 8 (over z, y).
Axes of the slice: x: 2, y: 2, z: 4, core: 2. Of those that a mesh axis runs over, the one named last changes fastest.
Arguments:
- tiles: float32 [4, 8, 128, 128, 128], P('row', 'col'), may hold values from -0.125 to 0.125
- tile_rows: int32 [4, 8, 128], P('row', 'col'), may hold values from 0 to 31, as said below
- tile_cols: int32 [4, 8, 128], P('row', 'col'), may hold values from 0 to 15, as said below
- tile_counts: int32 [4, 8], P('row', 'col'), may hold values from 1 to 128, as said below
- vectors: float32 [8, 16384], P(None, ('row', 'col')), may hold values from -6 to 6
Outputs:
- product: float32 [8, 16384], P(None, ('row', 'col'))
Inputs may be any that keep to these rules, and one draw needn't show every extreme that they name: `tile_counts`: each device has 1 to 128 live slots; the target count of grid row r is the ceiling of 128 * (r + 1) / 4 less a jitter of 0 to 32, at least 1; one device of the last grid row has exactly 128. `tile_rows`: live slots of a device name distinct tiles on or below the block diagonal (global block row at least global block column); slots past the count hold 0. `tile_cols`: drawn together with tile_rows; slots past the count hold 0.
All inputs are finite; a program needn't handle non-finite values.
Results may differ from a plain program's by a relative error of at most 0.0003.
Values sent between devices are 32-bit elements; how exact they have to be, the bound alone decides.
A program may use at most 64 MiB of HBM per device.

v0:
```python
import jax
import jax.numpy as jnp
from jax import lax
from jax.sharding import PartitionSpec as P


def tile_products(blocks, rows, cols, row_inputs, col_inputs):
    from_cols = jnp.take(col_inputs, cols, axis=1)
    from_rows = jnp.take(row_inputs, rows, axis=1)
    first = jnp.einsum("tab,ktb->kta", blocks, from_cols, precision=lax.Precision.HIGHEST)
    second = jnp.einsum("tab,kta->ktb", blocks, from_rows, precision=lax.Precision.HIGHEST)
    return (first, second)


def block_sums(terms, labels, valid, count):
    targets = jnp.arange(count, dtype=jnp.int32)
    hits = ((labels[:, None] == targets[None, :]) & valid[:, None]).astype(jnp.float32)
    return jnp.einsum("kta,ti->ika", terms, hits, precision=lax.Precision.HIGHEST)


def body(tiles, tile_rows, tile_cols, tile_counts, vectors):
    blocks = tiles[0, 0]
    rows = tile_rows[0, 0]
    cols = tile_cols[0, 0]
    count = tile_counts[0, 0]
    vector_count, width = vectors.shape
    tile_side = blocks.shape[1]
    row_devices = lax.axis_size("row")
    column_devices = lax.axis_size("col")
    local_blocks = width // tile_side
    row_blocks = column_devices * local_blocks
    col_blocks = row_devices * local_blocks
    valid = jnp.arange(blocks.shape[0], dtype=jnp.int32) < count
    col_inputs = lax.all_gather(vectors, "row", axis=1, tiled=True).reshape(
        vector_count, col_blocks, tile_side
    )
    row_inputs = lax.all_gather(vectors, "col", axis=1, tiled=True).reshape(
        vector_count, row_blocks, tile_side
    )
    first, second = tile_products(blocks, rows, cols, row_inputs, col_inputs)
    row_part = jnp.transpose(block_sums(first, rows, valid, row_blocks), (1, 0, 2))
    col_part = jnp.transpose(block_sums(second, cols, valid, col_blocks), (1, 0, 2))
    row_total = lax.psum_scatter(
        row_part.reshape(vector_count, row_blocks * tile_side),
        "col",
        scatter_dimension=1,
        tiled=True,
    )
    col_total = lax.psum_scatter(
        col_part.reshape(vector_count, col_blocks * tile_side),
        "row",
        scatter_dimension=1,
        tiled=True,
    )
    result = row_total + col_total
    return result


def solution(mesh):
    in_specs = (
        P("row", "col", None, None, None),
        P("row", "col", None),
        P("row", "col", None),
        P("row", "col"),
        P(None, ("row", "col")),
    )
    out_specs = P(None, ("row", "col"))
    return jax.shard_map(body, mesh=mesh, in_specs=in_specs, out_specs=out_specs, check_vma=False)
```

profile of v0, /device:TPU:0, one launch (start us, length us, event | category | flops | bytes accessed | tf_op | source)
XLA Modules:
  0.0 145.6 jit_solution(10243617955626819257)
XLA Ops:
  6.5 0.0 copy-start
  6.5 0.0 copy-start.1
  6.5 0.0 reduce-scatter.5.cloned.1.call-start
  6.5 0.7 fusion.27
  7.2 0.7 compare_and_fusion
  8.5 32.5 %all_gather.7 = f32[8,4096]{1,0:T(8,128)S(1)} all-gather(f32[8,512]{1,0:T(8,128)} %param.9), channel_id=1, replica_groups=mesh['row'=4,'col'=8] {'col'}, dimensions={1}, use_global_device_ids=true | all-gather | bytes 147456 | tf_op jit(solution)/shard_map/all_gather | solution.py:37
  41.1 0.8 gather_fusion.1
  41.8 0.0 copy-start.2
  41.9 9.4 %fusion = f32[128,8,128]{2,1,0:T(8,128)S(1)} fusion(f32[1,1,128,128,128]{4,3,2,1,0:T(8,128)} %param.5, f32[128,8,128]{2,1,0:T(8,128)S(1)} %gather_fusion.1, pred[128]{0:T(512)(128)(4,1)S(1)} %compare_and_fusion), kind=kOutput, calls=%fused_computation.2 | convolution fusion | flops 201457664 | bytes 9437312 | tf_op jit(solution)/shard_map/tab,kta->ktb/dot_general | solution.py:11
  51.3 0.0 copy-done.1
  51.3 0.3 convolution_bitcast_fusion.1
  51.6 0.6 copy.21
  52.2 0.0 reduce-scatter.5.cloned.1.call-update
  52.3 0.0 reduce-scatter.3.cloned.1.call-start
  52.3 0.0 copy-done
  52.3 5.2 %all_gather.6 = f32[8,2048]{1,0:T(8,128)S(1)} all-gather(f32[8,512]{1,0:T(8,128)S(1)} %copy-done), channel_id=1, replica_groups=mesh['row'=4,'col'=8] {'row'}, dimensions={1}, use_global_device_ids=true | all-gather | bytes 81920 | tf_op jit(solution)/shard_map/all_gather | solution.py:34
  57.6 0.8 gather_fusion
  58.4 15.5 %fusion.2 = f32[128,8,128]{2,1,0:T(8,128)S(1)} fusion(f32[1,1,128,128,128]{4,3,2,1,0:T(8,128)} %param.5, f32[128,8,128]{2,1,0:T(8,128)S(1)} %gather_fusion, pred[128]{0:T(512)(128)(4,1)S(1)} %compare_and_fusion.1), kind=kOutput, calls=%fused_computation.4 | convolution fusion | flops 201457664 | bytes 9437312 | tf_op jit(solution)/shard_map/tab,ktb->kta/dot_general | solution.py:10
  73.9 0.0 copy-done.2
  73.9 0.4 convolution_bitcast_fusion
  74.2 0.7 copy.20
  75.0 0.0 reduce-scatter.3.cloned.1.call-update
  75.0 0.0 reduce-scatter.5.cloned.1.call-done
  75.0 62.4 %reduce-scatter.3.cloned.1.call-done = f32[8,512]{1,0:T(8,128)} async-done(((f32[8,4096]{1,0:T(8,128)}), f32[8,512]{1,0:T(8,128)}) %reduce-scatter.3.cloned.1.call-update) | async-done | bytes 16400 | tf_op jit(solution)/shard_map/reduce_scatter | solution.py:43
  137.4 1.3 add.57
  (5 shorter events, 0.0 us)
Async XLA Ops:
  6.5 45.8 %copy-start = (f32[8,512]{1,0:T(8,128)S(1)}, f32[8,512]{1,0:T(8,128)}, u32[]{:S(2)}) copy-start(f32[8,512]{1,0:T(8,128)} %param.9) | copy-start | bytes 49156
  6.5 44.7 %copy-start.1 = (s32[1,1,128]{2,1,0:T(1,128)S(1)}, s32[1,1,128]{2,1,0:T(1,128)}, u32[]{:S(2)}) copy-start(s32[1,1,128]{2,1,0:T(1,128)} %param.7) | copy-start | bytes 1540
  6.5 68.5 %reduce-scatter.5.cloned.1.call-start = ((), (), s32[]{:S(2)}) async-start(), calls=%async_computation.3 | async-start | bytes 81920 | tf_op jit(solution)/shard_map/reduce_scatter | solution.py:49
  41.8 32.0 %copy-start.2 = (s32[1,1,128]{2,1,0:T(1,128)S(1)}, s32[1,1,128]{2,1,0:T(1,128)}, u32[]{:S(2)}) copy-start(s32[1,1,128]{2,1,0:T(1,128)} %param.6) | copy-start | bytes 1540
  52.3 85.1 %reduce-scatter.3.cloned.1.call-start = ((), (), s32[]{:S(2)}) async-start(), calls=%async_computation.2 | async-start | bytes 147456 | tf_op jit(solution)/shard_map/reduce_scatter | solution.py:43
Sparse Core Ops, SparseCore 0:
  52.4 20.3 reduce-scatter.4
  76.5 60.8 reduce-scatter.2
where the time goes:
time: 146 us
  waiting for transfers between devices  62.4 us (43%)
  blocking collectives  37.8 us (26%)
  matrix products  25.6 us (18%)
  between operations  14.1 us (10%)
  local copies, waits for them, and re-layouts  2.9 us (2%)
  other arithmetic  2.71 us (2%)
    reduce_scatter x1, waiting for transfers between devices, body(): lax.psum_scatter(row_part.reshape(vector_count, row_blocks * tile_side),...  62.4 us
    all_gather x1, blocking collectives, body(): lax.all_gather(vectors, 'col', axis=1, tiled=True)  32.5 us
    dot_general x1, matrix products, tile_products(): jnp.einsum('tab,ktb->kta', blocks, from_cols, precision=lax.Precision.HIG...  15.5 us
    dot_general x1, matrix products, tile_products(): jnp.einsum('tab,kta->ktb', blocks, from_rows, precision=lax.Precision.HIG...  9.4 us
    all_gather x1, blocking collectives, body(): lax.all_gather(vectors, 'row', axis=1, tiled=True)  5.25 us
  transfers between devices with their start and end apart: 2, of which 1 were waited for; matrix products, arithmetic and copies ran while one was open for 12% of the time, Pallas kernels for 0%

commit v1 on v0

v1 whole, which is shorter than its diff:
```python
import functools

import jax
import jax.numpy as jnp
from jax import lax
from jax.experimental import pallas as pl
from jax.experimental.pallas import tpu as pltpu
from jax.sharding import PartitionSpec as P

MESH = pl.DeviceIdType.MESH
F32 = jnp.float32
BF16 = jnp.bfloat16
CHUNKS = 8
UNROLL = 4


def split(value):
    high = value.astype(BF16)
    low = (value - high.astype(F32)).astype(BF16)
    return high, low


def hit_matrix(labels, count, blocks, vecs):
    slots = labels.shape[1]
    slot = lax.broadcasted_iota(jnp.int32, (vecs, slots), 1)
    names = jnp.where(slot < count, jnp.broadcast_to(labels, (vecs, slots)), -1)
    source = lax.broadcasted_iota(jnp.int32, (slots, slots * vecs), 0)
    target = lax.broadcasted_iota(jnp.int32, (slots, slots * vecs), 1)
    spread = jnp.where((target >= source * vecs) & (target < source * vecs + vecs), 1.0, 0.0).astype(BF16)
    wide = jnp.dot(names.astype(F32).astype(BF16), spread, preferred_element_type=F32)[0:1]
    lane = lax.rem(lax.broadcasted_iota(jnp.int32, (1, slots * vecs), 1), vecs)
    code = wide.astype(jnp.int32) * vecs + lane
    place = lax.broadcasted_iota(jnp.int32, (blocks * vecs, slots * vecs), 0)
    return jnp.where(place == code, 1.0, 0.0).astype(BF16)


def kernel(
    rows_s, cols_s, count_s, rows_v, cols_v, x_ref, tiles_ref, out_ref,
    raw, both, col_x, row_x, col_lhs, row_lhs, row_hits, col_hits, terms, row_part, col_part, row_in, col_in,
    tile_sem, colx_send, colx_recv, rowx_send, rowx_recv, rowp_send, rowp_recv, colp_send, colp_recv,
):
    row_devices = lax.axis_size("row")
    column_devices = lax.axis_size("col")
    r = lax.axis_index("row")
    c = lax.axis_index("col")
    vecs, width = x_ref.shape
    slots, side, _ = tiles_ref.shape
    local = width // side
    row_blocks = column_devices * local
    col_blocks = row_devices * local
    chunk = slots // CHUNKS

    fetches = []
    for n in range(CHUNKS):
        piece = pl.ds(n * chunk, chunk)
        fetch = pltpu.make_async_copy(tiles_ref.at[piece], raw.at[piece], tile_sem.at[n])
        fetch.start()
        fetches.append(fetch)

    row_peers = [(lax.rem(r + d, row_devices), c) for d in range(1, row_devices)]
    col_peers = [(r, lax.rem(c + d, column_devices)) for d in range(1, column_devices)]

    barrier = pltpu.get_barrier_semaphore()
    for peer in row_peers + col_peers:
        pl.semaphore_signal(barrier, inc=1, device_id=peer, device_id_type=MESH)
    pl.semaphore_wait(barrier, len(row_peers) + len(col_peers))

    colx, rowx = [], []
    for n, peer in enumerate(row_peers):
        colx.append(pltpu.make_async_remote_copy(
            src_ref=x_ref, dst_ref=col_x.at[r], send_sem=colx_send.at[n], recv_sem=colx_recv.at[n],
            device_id=peer, device_id_type=MESH))
        colx[-1].start()
    for n, peer in enumerate(col_peers):
        rowx.append(pltpu.make_async_remote_copy(
            src_ref=x_ref, dst_ref=row_x.at[c], send_sem=rowx_send.at[n], recv_sem=rowx_recv.at[n],
            device_id=peer, device_id_type=MESH))
        rowx[-1].start()
    col_x[r] = x_ref[...]
    row_x[c] = x_ref[...]

    count = count_s[0, 0]
    row_hits[...] = hit_matrix(rows_v[...], count, row_blocks, vecs)
    col_hits[...] = hit_matrix(cols_v[...], count, col_blocks, vecs)

    for n in range(CHUNKS):
        fetches[n].wait()

        def halve(t, carry):
            high, low = split(raw[t])
            place = pl.ds(pl.multiple_of(t * side, side), side)
            both[place, 0:side] = high
            both[place, side:] = low
            return carry

        lax.fori_loop(n * chunk, (n + 1) * chunk, halve, 0, unroll=2)

    for copy in colx:
        copy.wait()
    for i in range(row_devices):
        for j in range(local):
            high, low = split(col_x[i, :, j * side:(j + 1) * side])
            n = i * local + j
            upper = jnp.concatenate([high, low], axis=0)
            under = jnp.concatenate([high, jnp.zeros_like(low)], axis=0)
            col_lhs[n, :, 0:side] = upper
            col_lhs[n, :, side:] = under

    def add_up(hits):
        high, low = split(terms[...])
        total = jnp.dot(hits[...], jnp.concatenate([high, low], axis=1), preferred_element_type=F32)
        return total[:, 0:side] + total[:, side:]

    def first(step, carry):
        for u in range(UNROLL):
            pair = step * UNROLL + u
            lhs = jnp.concatenate([col_lhs[cols_s[0, 2 * pair]], col_lhs[cols_s[0, 2 * pair + 1]]], axis=0)
            rhs = both[pl.ds(pl.multiple_of(pair * 2 * side, 2 * side), 2 * side), :]
            got = lax.dot_general(lhs, rhs, (((1,), (1,)), ((), ())), preferred_element_type=F32)
            left = got[0:2 * vecs, 0:side]
            right = got[2 * vecs:, side:]
            place = pl.multiple_of(pair * 2 * vecs, 2 * vecs)
            terms[pl.ds(place, vecs), :] = left[0:vecs] + left[vecs:]
            terms[pl.ds(place + vecs, vecs), :] = right[0:vecs] + right[vecs:]
        return carry

    lax.fori_loop(0, slots // (2 * UNROLL), first, 0)
    row_part[...] = add_up(row_hits).reshape(row_blocks, vecs, side)
    rowp = []
    for n, peer in enumerate(col_peers):
        rowp.append(pltpu.make_async_remote_copy(
            src_ref=row_part.at[pl.ds(peer[1] * local, local)], dst_ref=row_in.at[n],
            send_sem=rowp_send.at[n], recv_sem=rowp_recv.at[n], device_id=peer, device_id_type=MESH))
        rowp[-1].start()

    for copy in rowx:
        copy.wait()
    for i in range(column_devices):
        for j in range(local):
            high, low = split(row_x[i, :, j * side:(j + 1) * side])
            row_lhs[i * local + j] = jnp.concatenate([high, low], axis=0)

    def second(step, carry):
        blank = jnp.zeros((2 * vecs, side), BF16)
        for u in range(UNROLL):
            pair = step * UNROLL + u
            one = row_lhs[rows_s[0, 2 * pair]]
            two = row_lhs[rows_s[0, 2 * pair + 1]]
            lhs = jnp.concatenate([
                jnp.concatenate([one, blank], axis=1),
                jnp.concatenate([blank, two], axis=1),
            ], axis=0)
            rhs = both[pl.ds(pl.multiple_of(pair * 2 * side, 2 * side), 2 * side), :]
            got = jnp.dot(lhs, rhs, preferred_element_type=F32)
            got = got[:, 0:side] + got[:, side:]
            place = pl.multiple_of(pair * 2 * vecs, 2 * vecs)
            terms[pl.ds(place, vecs), :] = got[0:vecs] + got[vecs:2 * vecs]
            terms[pl.ds(place + vecs, vecs), :] = got[2 * vecs:3 * vecs] + got[3 * vecs:]
        return carry

    lax.fori_loop(0, slots // (2 * UNROLL), second, 0)
    col_part[...] = add_up(col_hits).reshape(col_blocks, vecs, side)
    colp = []
    for n, peer in enumerate(row_peers):
        colp.append(pltpu.make_async_remote_copy(
            src_ref=col_part.at[pl.ds(peer[0] * local, local)], dst_ref=col_in.at[n],
            send_sem=colp_send.at[n], recv_sem=colp_recv.at[n], device_id=peer, device_id_type=MESH))
        colp[-1].start()

    total = row_part[pl.ds(c * local, local)] + col_part[pl.ds(r * local, local)]
    for n, copy in enumerate(rowp):
        copy.wait()
        total += row_in[n]
    for n, copy in enumerate(colp):
        copy.wait()
        total += col_in[n]
    for j in range(local):
        out_ref[:, j * side:(j + 1) * side] = total[j]


def body(tiles, tile_rows, tile_cols, tile_counts, vectors):
    vecs, width = vectors.shape
    slots, side = tiles.shape[2:4]
    row_devices = lax.axis_size("row")
    column_devices = lax.axis_size("col")
    local = width // side
    row_blocks = column_devices * local
    col_blocks = row_devices * local
    rows = tile_rows.reshape(1, slots)
    cols = tile_cols.reshape(1, slots)
    vmem = pl.BlockSpec(memory_space=pltpu.VMEM)
    smem = pl.BlockSpec(memory_space=pltpu.SMEM)
    dma = pltpu.SemaphoreType.DMA
    return pl.pallas_call(
        kernel,
        out_shape=jax.ShapeDtypeStruct((vecs, width), F32),
        in_specs=[smem, smem, smem, vmem, vmem, vmem, pl.BlockSpec(memory_space=pl.ANY)],
        out_specs=vmem,
        scratch_shapes=[
            pltpu.VMEM((slots, side, side), F32),
            pltpu.VMEM((slots * side, 2 * side), BF16),
            pltpu.VMEM((row_devices, vecs, width), F32),
            pltpu.VMEM((column_devices, vecs, width), F32),
            pltpu.VMEM((col_blocks, 2 * vecs, 2 * side), BF16),
            pltpu.VMEM((row_blocks, 2 * vecs, side), BF16),
            pltpu.VMEM((row_blocks * vecs, slots * vecs), BF16),
            pltpu.VMEM((col_blocks * vecs, slots * vecs), BF16),
            pltpu.VMEM((slots * vecs, side), F32),
            pltpu.VMEM((row_blocks, vecs, side), F32),
            pltpu.VMEM((col_blocks, vecs, side), F32),
            pltpu.VMEM((column_devices - 1, local, vecs, side), F32),
            pltpu.VMEM((row_devices - 1, local, vecs, side), F32),
            dma((CHUNKS,)),
            dma((row_devices - 1,)),
            dma((row_devices - 1,)),
            dma((column_devices - 1,)),
            dma((column_devices - 1,)),
            dma((column_devices - 1,)),
            dma((column_devices - 1,)),
            dma((row_devices - 1,)),
            dma((row_devices - 1,)),
        ],
        compiler_params=pltpu.CompilerParams(
            collective_id=0, has_side_effects=True, vmem_limit_bytes=56 * 2**20
        ),
        cost_estimate=pl.CostEstimate(
            flops=12 * slots * side * side * vecs, bytes_accessed=4 * slots * side * side, transcendentals=0
        ),
        name="symmetric_product",
    )(rows, cols, tile_counts, rows, cols, vectors, tiles.reshape(slots, side, side))


def solution(mesh):
    in_specs = (
        P("row", "col", None, None, None),
        P("row", "col", None),
        P("row", "col", None),
        P("row", "col"),
        P(None, ("row", "col")),
    )
    out_specs = P(None, ("row", "col"))
    return jax.shard_map(body, mesh=mesh, in_specs=in_specs, out_specs=out_specs, check_vma=False)
```

time: 146 us -> 23.9 us (0.16)
  waiting for transfers between devices: 62.4 us -> 0 us
  blocking collectives: 37.8 us -> 0 us
  matrix products: 25.6 us -> 0 us
  Pallas kernels: 0 us -> 21.6 us
  between operations: 14.1 us -> 0.66 us
  other arithmetic: 2.71 us -> 0 us
  local copies, waits for them, and re-layouts: 2.9 us -> 1.32 us
    reduce_scatter x2 -> x0, waiting for transfers between devices: 62.4 us -> none  [the longest x1 62.4 us: body(): lax.psum_scatter(row_part.reshape(vector_count, row_blocks * tile_side),...]
    all_gather x2 -> x0, blocking collectives: 37.8 us -> none  [the longest x1 32.5 us: body(): lax.all_gather(vectors, 'col', axis=1, tiled=True)]
    dot_general x4 -> x0, matrix products: 25.6 us -> none  [the longest x1 15.5 us: tile_products(): jnp.einsum('tab,ktb->kta', blocks, from_cols, precision=lax.Precision.HIG...]
    pallas_call x0 -> x1, Pallas kernels: none -> 21.6 us  [body(): pl.pallas_call(kernel, out_shape=jax.ShapeDtypeStruct((vecs, width), F32)...]
    gather x2 -> x0, local copies, waits for them, and re-layouts: 1.52 us -> none  [the longest x1 0.76 us: tile_products(): from_cols = jnp.take(col_inputs, cols, axis=1)]
  transfers between devices with their start and end apart: 2 -> 0, of which waited for: 1 -> 0; matrix products, arithmetic and copies ran while one was open for 12% -> 0% of each run, Pallas kernels for 0% -> 0%
where the time goes in v1:
time: 23.9 us; the launch traced here: 23.6 us
  Pallas kernels  21.6 us (90%)
  local copies, waits for them, and re-layouts  1.32 us (6%)
  between operations  0.66 us (3%)
    pallas_call x1, Pallas kernels, body(): pl.pallas_call(kernel, out_shape=jax.ShapeDtypeStruct((vecs, width), F32)...  21.6 us
    unnamed x1, local copies, waits for them, and re-layouts  1.32 us

profile of v1, /device:TPU:0, one launch (start us, length us, event | category | flops | bytes accessed | tf_op | source)
XLA Modules:
  0.0 23.6 jit_solution(16729018595508356343)
XLA Ops:
  0.7 21.6 %symmetric_product.1 = f32[8,512]{1,0:T(8,128)} custom-call(s32[1,128]{1,0:T(1,128)} %bitcast.4, s32[1,128]{1,0:T(1,128)} %bitcast.6, s32[1,1]{1,0:T(1,128)S(6)} %copy.7.count_s, s32[1,128]{1,0:T(1,128)} %bitcast.5, s32[1,128]{1,0:T(1,128)} %bitcast.7, f32[8,512]{1,0:T(8,128)} %x_ref.1, f32[128,128,128]{2,1,0:T(8,128)} %bitcast.3), custom_call_target="tpu_custom_call" | custom-call | flops 201326592 | bytes 8388608 | tf_op jit(solution)/shard_map/symmetric_product/pallas_call | solution.py:194
  22.3 1.3 %copy.8 = f32[8,512]{1,0:T(8,128)} copy(f32[8,512]{1,0:T(8,128)} %symmetric_product.1) | data formatting | bytes 32768

commit v2 on v1

--- a/solution.py
+++ b/solution.py
@@ -11,7 +11,7 @@
 F32 = jnp.float32
 BF16 = jnp.bfloat16
 CHUNKS = 8
-UNROLL = 4
+UNROLL = 16
 
 
 def split(value):
@@ -35,9 +35,9 @@
 
 
 def kernel(
-    rows_s, cols_s, count_s, rows_v, cols_v, x_ref, tiles_ref, out_ref,
-    raw, both, col_x, row_x, col_lhs, row_lhs, row_hits, col_hits, terms, row_part, col_part, row_in, col_in,
-    tile_sem, colx_send, colx_recv, rowx_send, rowx_recv, rowp_send, rowp_recv, colp_send, colp_recv,
+    rows_ref, cols_ref, count_ref, x_ref, tiles_ref, out_ref,
+    rows_s, cols_s, count_s, rows_v, cols_v, raw, both, col_x, row_x, col_lhs, row_lhs, row_hits, col_hits, terms, row_part, col_part, row_in, col_in,
+    small_sem, tile_sem, colx_send, colx_recv, rowx_send, rowx_recv, rowp_send, rowp_recv, colp_send, colp_recv,
 ):
     row_devices = lax.axis_size("row")
     column_devices = lax.axis_size("col")
@@ -50,19 +50,28 @@
     col_blocks = row_devices * local
     chunk = slots // CHUNKS
 
+    row_peers = [(lax.rem(r + d, row_devices), c) for d in range(1, row_devices)]
+    col_peers = [(r, lax.rem(c + d, column_devices)) for d in range(1, column_devices)]
+
+    barrier = pltpu.get_barrier_semaphore()
+    for peer in row_peers + col_peers:
+        pl.semaphore_signal(barrier, inc=1, device_id=peer, device_id_type=MESH)
+
+    smalls = [
+        pltpu.make_async_copy(source, target, small_sem.at[n])
+        for n, (source, target) in enumerate([
+            (rows_ref, rows_v), (cols_ref, cols_v), (count_ref, count_s), (rows_ref, rows_s), (cols_ref, cols_s),
+            (x_ref, col_x.at[r]), (x_ref, row_x.at[c]),
+        ])
+    ]
+    for copy in smalls:
+        copy.start()
     fetches = []
     for n in range(CHUNKS):
         piece = pl.ds(n * chunk, chunk)
         fetch = pltpu.make_async_copy(tiles_ref.at[piece], raw.at[piece], tile_sem.at[n])
         fetch.start()
         fetches.append(fetch)
-
-    row_peers = [(lax.rem(r + d, row_devices), c) for d in range(1, row_devices)]
-    col_peers = [(r, lax.rem(c + d, column_devices)) for d in range(1, column_devices)]
-
-    barrier = pltpu.get_barrier_semaphore()
-    for peer in row_peers + col_peers:
-        pl.semaphore_signal(barrier, inc=1, device_id=peer, device_id_type=MESH)
     pl.semaphore_wait(barrier, len(row_peers) + len(col_peers))
 
     colx, rowx = [], []
@@ -76,9 +85,8 @@
             src_ref=x_ref, dst_ref=row_x.at[c], send_sem=rowx_send.at[n], recv_sem=rowx_recv.at[n],
             device_id=peer, device_id_type=MESH))
         rowx[-1].start()
-    col_x[r] = x_ref[...]
-    row_x[c] = x_ref[...]
-
+    for copy in smalls:
+        copy.wait()
     count = count_s[0, 0]
     row_hits[...] = hit_matrix(rows_v[...], count, row_blocks, vecs)
     col_hits[...] = hit_matrix(cols_v[...], count, col_blocks, vecs)
@@ -93,7 +101,7 @@
             both[place, side:] = low
             return carry
 
-        lax.fori_loop(n * chunk, (n + 1) * chunk, halve, 0, unroll=2)
+        lax.fori_loop(n * chunk, (n + 1) * chunk, halve, 0, unroll=8)
 
     for copy in colx:
         copy.wait()
@@ -189,14 +197,18 @@
     rows = tile_rows.reshape(1, slots)
     cols = tile_cols.reshape(1, slots)
     vmem = pl.BlockSpec(memory_space=pltpu.VMEM)
-    smem = pl.BlockSpec(memory_space=pltpu.SMEM)
     dma = pltpu.SemaphoreType.DMA
     return pl.pallas_call(
         kernel,
-        out_shape=jax.ShapeDtypeStruct((vecs, width), F32),
-        in_specs=[smem, smem, smem, vmem, vmem, vmem, pl.BlockSpec(memory_space=pl.ANY)],
+        out_shape=pltpu.VMEM((vecs, width), F32),
+        in_specs=[pl.BlockSpec(memory_space=pltpu.HBM)] * 5,
         out_specs=vmem,
         scratch_shapes=[
+            pltpu.SMEM((1, slots), jnp.int32),
+            pltpu.SMEM((1, slots), jnp.int32),
+            pltpu.SMEM((1, 1), jnp.int32),
+            pltpu.VMEM((1, slots), jnp.int32),
+            pltpu.VMEM((1, slots), jnp.int32),
             pltpu.VMEM((slots, side, side), F32),
             pltpu.VMEM((slots * side, 2 * side), BF16),
             pltpu.VMEM((row_devices, vecs, width), F32),
@@ -210,6 +222,7 @@
             pltpu.VMEM((col_blocks, vecs, side), F32),
             pltpu.VMEM((column_devices - 1, local, vecs, side), F32),
             pltpu.VMEM((row_devices - 1, local, vecs, side), F32),
+            dma((7,)),
             dma((CHUNKS,)),
             dma((row_devices - 1,)),
             dma((row_devices - 1,)),
@@ -227,7 +240,7 @@
             flops=12 * slots * side * side * vecs, bytes_accessed=4 * slots * side * side, transcendentals=0
         ),
         name="symmetric_product",
-    )(rows, cols, tile_counts, rows, cols, vectors, tiles.reshape(slots, side, side))
+    )(rows, cols, tile_counts, vectors, tiles.reshape(slots, side, side))
 
 
 def solution(mesh):

time: 23.9 us -> 19.1 us (0.80)
  Pallas kernels: 21.6 us -> 17.7 us
  local copies, waits for them, and re-layouts: 1.32 us -> 0.61 us
    pallas_call x1, Pallas kernels: 21.6 us -> 17.7 us  [body(): pl.pallas_call(kernel, out_shape=pltpu.VMEM((vecs, width), F32), in_specs...]
    unnamed x1, local copies, waits for them, and re-layouts: 1.32 us -> 0.61 us
where the time goes in v2:
time: 19.1 us; the launch traced here: 19 us
  Pallas kernels  17.7 us (93%)
  between operations  0.66 us (3%)
  local copies, waits for them, and re-layouts  0.61 us (3%)
    pallas_call x1, Pallas kernels, body(): pl.pallas_call(kernel, out_shape=pltpu.VMEM((vecs, width), F32), in_specs...  17.7 us
    unnamed x1, local copies, waits for them, and re-layouts  0.61 us

profile of v2, /device:TPU:0, one launch (start us, length us, event | category | flops | bytes accessed | tf_op | source)
XLA Modules:
  0.0 19.0 jit_solution(7417414519270223553)
XLA Ops:
  0.7 17.7 %symmetric_product.1 = f32[8,512]{1,0:T(8,128)S(1)} custom-call(s32[1,128]{1,0:T(1,128)} %bitcast.4, s32[1,128]{1,0:T(1,128)} %bitcast.5, s32[1,1]{1,0:T(1,128)S(6)} %copy.8.count_ref, f32[8,512]{1,0:T(8,128)} %x_ref.1, f32[128,128,128]{2,1,0:T(8,128)} %bitcast.3), custom_call_target="tpu_custom_call" | custom-call | flops 201326592 | bytes 8388608 | tf_op jit(solution)/shard_map/symmetric_product/pallas_call | solution.py:201
  18.3 0.6 %copy.7 = f32[8,512]{1,0:T(8,128)} copy(f32[8,512]{1,0:T(8,128)S(1)} %symmetric_product.1) | data formatting | bytes 32768

commit v3 on v2

--- a/solution.py
+++ b/solution.py
@@ -11,7 +11,8 @@
 F32 = jnp.float32
 BF16 = jnp.bfloat16
 CHUNKS = 8
-UNROLL = 16
+GROUP = 4
+UNROLL = 8
 
 
 def split(value):
@@ -121,18 +122,17 @@
 
     def first(step, carry):
         for u in range(UNROLL):
-            pair = step * UNROLL + u
-            lhs = jnp.concatenate([col_lhs[cols_s[0, 2 * pair]], col_lhs[cols_s[0, 2 * pair + 1]]], axis=0)
-            rhs = both[pl.ds(pl.multiple_of(pair * 2 * side, 2 * side), 2 * side), :]
+            quad = step * UNROLL + u
+            lhs = jnp.concatenate([col_lhs[cols_s[0, GROUP * quad + q]] for q in range(GROUP)], axis=0)
+            rhs = both[pl.ds(pl.multiple_of(quad * GROUP * side, GROUP * side), GROUP * side), :]
             got = lax.dot_general(lhs, rhs, (((1,), (1,)), ((), ())), preferred_element_type=F32)
-            left = got[0:2 * vecs, 0:side]
-            right = got[2 * vecs:, side:]
-            place = pl.multiple_of(pair * 2 * vecs, 2 * vecs)
-            terms[pl.ds(place, vecs), :] = left[0:vecs] + left[vecs:]
-            terms[pl.ds(place + vecs, vecs), :] = right[0:vecs] + right[vecs:]
+            place = pl.multiple_of(quad * GROUP * vecs, GROUP * vecs)
+            for q in range(GROUP):
+                own = got[2 * q * vecs:2 * (q + 1) * vecs, q * side:(q + 1) * side]
+                terms[pl.ds(place + q * vecs, vecs), :] = own[0:vecs] + own[vecs:]
         return carry
 
-    lax.fori_loop(0, slots // (2 * UNROLL), first, 0)
+    lax.fori_loop(0, slots // (GROUP * UNROLL), first, 0)
     row_part[...] = add_up(row_hits).reshape(row_blocks, vecs, side)
     rowp = []
     for n, peer in enumerate(col_peers):
@@ -151,22 +151,26 @@
     def second(step, carry):
         blank = jnp.zeros((2 * vecs, side), BF16)
         for u in range(UNROLL):
-            pair = step * UNROLL + u
-            one = row_lhs[rows_s[0, 2 * pair]]
-            two = row_lhs[rows_s[0, 2 * pair + 1]]
+            quad = step * UNROLL + u
+            parts = [row_lhs[rows_s[0, GROUP * quad + q]] for q in range(GROUP)]
             lhs = jnp.concatenate([
-                jnp.concatenate([one, blank], axis=1),
-                jnp.concatenate([blank, two], axis=1),
+                jnp.concatenate([part, blank] if q % 2 == 0 else [blank, part], axis=1)
+                for q, part in enumerate(parts)
             ], axis=0)
-            rhs = both[pl.ds(pl.multiple_of(pair * 2 * side, 2 * side), 2 * side), :]
+            start = pl.multiple_of(quad * GROUP * side, GROUP * side)
+            rhs = jnp.concatenate([
+                both[pl.ds(start + 2 * h * side, 2 * side), :] for h in range(GROUP // 2)
+            ], axis=1)
             got = jnp.dot(lhs, rhs, preferred_element_type=F32)
-            got = got[:, 0:side] + got[:, side:]
-            place = pl.multiple_of(pair * 2 * vecs, 2 * vecs)
-            terms[pl.ds(place, vecs), :] = got[0:vecs] + got[vecs:2 * vecs]
-            terms[pl.ds(place + vecs, vecs), :] = got[2 * vecs:3 * vecs] + got[3 * vecs:]
+            place = pl.multiple_of(quad * GROUP * vecs, GROUP * vecs)
+            for q in range(GROUP):
+                h = q // 2
+                own = got[2 * q * vecs:2 * (q + 1) * vecs, 2 * h * side:2 * (h + 1) * side]
+                own = own[0:vecs] + own[vecs:]
+                terms[pl.ds(place + q * vecs, vecs), :] = own[:, 0:side] + own[:, side:]
         return carry
 
-    lax.fori_loop(0, slots // (2 * UNROLL), second, 0)
+    lax.fori_loop(0, slots // (GROUP * UNROLL), second, 0)
     col_part[...] = add_up(col_hits).reshape(col_blocks, vecs, side)
     colp = []
     for n, peer in enumerate(row_peers):

time: 19.1 us -> 19.3 us (1.010)
  Pallas kernels: 17.7 us -> 17.9 us
    pallas_call x1, Pallas kernels: 17.7 us -> 17.9 us  [body(): pl.pallas_call(kernel, out_shape=pltpu.VMEM((vecs, width), F32), in_specs...]
where the time goes in v3:
time: 19.3 us; the launch traced here: 19.2 us
  Pallas kernels  17.9 us (93%)
  between operations  0.66 us (3%)
  local copies, waits for them, and re-layouts  0.61 us (3%)
    pallas_call x1, Pallas kernels, body(): pl.pallas_call(kernel, out_shape=pltpu.VMEM((vecs, width), F32), in_specs...  17.9 us
    unnamed x1, local copies, waits for them, and re-layouts  0.61 us

profile of v3, /device:TPU:0, one launch (start us, length us, event | category | flops | bytes accessed | tf_op | source)
XLA Modules:
  0.0 19.2 jit_solution(17201859447323514510)
XLA Ops:
  0.7 17.9 %symmetric_product.1 = f32[8,512]{1,0:T(8,128)S(1)} custom-call(s32[1,128]{1,0:T(1,128)} %bitcast.4, s32[1,128]{1,0:T(1,128)} %bitcast.5, s32[1,1]{1,0:T(1,128)S(6)} %copy.8.count_ref, f32[8,512]{1,0:T(8,128)} %x_ref.1, f32[128,128,128]{2,1,0:T(8,128)} %bitcast.3), custom_call_target="tpu_custom_call" | custom-call | flops 201326592 | bytes 8388608 | tf_op jit(solution)/shard_map/symmetric_product/pallas_call | solution.py:205
  18.6 0.6 %copy.7 = f32[8,512]{1,0:T(8,128)} copy(f32[8,512]{1,0:T(8,128)S(1)} %symmetric_product.1) | data formatting | bytes 32768

commit v4 on v3

--- a/solution.py
+++ b/solution.py
@@ -11,8 +11,8 @@
 F32 = jnp.float32
 BF16 = jnp.bfloat16
 CHUNKS = 8
-GROUP = 4
-UNROLL = 8
+GROUP = 2
+UNROLL = 16
 
 
 def split(value):
@@ -21,23 +21,17 @@
     return high, low
 
 
-def hit_matrix(labels, count, blocks, vecs):
+def hit_matrix(labels, count, blocks):
     slots = labels.shape[1]
-    slot = lax.broadcasted_iota(jnp.int32, (vecs, slots), 1)
-    names = jnp.where(slot < count, jnp.broadcast_to(labels, (vecs, slots)), -1)
-    source = lax.broadcasted_iota(jnp.int32, (slots, slots * vecs), 0)
-    target = lax.broadcasted_iota(jnp.int32, (slots, slots * vecs), 1)
-    spread = jnp.where((target >= source * vecs) & (target < source * vecs + vecs), 1.0, 0.0).astype(BF16)
-    wide = jnp.dot(names.astype(F32).astype(BF16), spread, preferred_element_type=F32)[0:1]
-    lane = lax.rem(lax.broadcasted_iota(jnp.int32, (1, slots * vecs), 1), vecs)
-    code = wide.astype(jnp.int32) * vecs + lane
-    place = lax.broadcasted_iota(jnp.int32, (blocks * vecs, slots * vecs), 0)
-    return jnp.where(place == code, 1.0, 0.0).astype(BF16)
+    slot = lax.broadcasted_iota(jnp.int32, (blocks, slots), 1)
+    block = lax.broadcasted_iota(jnp.int32, (blocks, slots), 0)
+    hits = jnp.where((slot < count) & (block == jnp.broadcast_to(labels, (blocks, slots))), 1.0, 0.0).astype(BF16)
+    return jnp.concatenate([hits, hits], axis=1)
 
 
 def kernel(
     rows_ref, cols_ref, count_ref, x_ref, tiles_ref, out_ref,
-    rows_s, cols_s, count_s, rows_v, cols_v, raw, both, col_x, row_x, col_lhs, row_lhs, row_hits, col_hits, terms, row_part, col_part, row_in, col_in,
+    rows_s, cols_s, count_s, rows_v, cols_v, raw, both, col_x, row_x, col_lhs, row_lhs, terms, row_part, col_part, row_in, col_in,
     small_sem, tile_sem, colx_send, colx_recv, rowx_send, rowx_recv, rowp_send, rowp_recv, colp_send, colp_recv,
 ):
     row_devices = lax.axis_size("row")
@@ -50,6 +44,11 @@
     row_blocks = column_devices * local
     col_blocks = row_devices * local
     chunk = slots // CHUNKS
+    stride = GROUP * UNROLL
+    span = local * vecs
+    most = (slots * (r + 1) + row_devices - 1) // row_devices
+    steps = (most + stride - 1) // stride
+    chunks = steps * (stride // chunk)
 
     row_peers = [(lax.rem(r + d, row_devices), c) for d in range(1, row_devices)]
     col_peers = [(r, lax.rem(c + d, column_devices)) for d in range(1, column_devices)]
@@ -67,12 +66,16 @@
     ]
     for copy in smalls:
         copy.start()
-    fetches = []
-    for n in range(CHUNKS):
+
+    def fetch(n):
         piece = pl.ds(n * chunk, chunk)
-        fetch = pltpu.make_async_copy(tiles_ref.at[piece], raw.at[piece], tile_sem.at[n])
-        fetch.start()
-        fetches.append(fetch)
+        return pltpu.make_async_copy(tiles_ref.at[piece], raw.at[piece], tile_sem.at[n])
+
+    def begin(n, carry):
+        fetch(n).start()
+        return carry
+
+    lax.fori_loop(0, chunks, begin, 0)
     pl.semaphore_wait(barrier, len(row_peers) + len(col_peers))
 
     colx, rowx = [], []
@@ -88,21 +91,26 @@
         rowx[-1].start()
     for copy in smalls:
         copy.wait()
-    count = count_s[0, 0]
-    row_hits[...] = hit_matrix(rows_v[...], count, row_blocks, vecs)
-    col_hits[...] = hit_matrix(cols_v[...], count, col_blocks, vecs)
-
-    for n in range(CHUNKS):
-        fetches[n].wait()
-
-        def halve(t, carry):
+    terms[...] = jnp.zeros_like(terms)
+
+    def halve(n, carry):
+        fetch(n).wait()
+
+        def one(i, carry):
+            t = n * chunk + i
             high, low = split(raw[t])
             place = pl.ds(pl.multiple_of(t * side, side), side)
             both[place, 0:side] = high
             both[place, side:] = low
             return carry
 
-        lax.fori_loop(n * chunk, (n + 1) * chunk, halve, 0, unroll=8)
+        return lax.fori_loop(0, chunk, one, carry, unroll=8)
+
+    lax.fori_loop(0, chunks, halve, 0)
+
+    count = count_s[0, 0]
+    row_hits = hit_matrix(rows_v[...], count, row_blocks)
+    col_hits = hit_matrix(cols_v[...], count, col_blocks)
 
     for copy in colx:
         copy.wait()
@@ -115,10 +123,14 @@
             col_lhs[n, :, 0:side] = upper
             col_lhs[n, :, side:] = under
 
-    def add_up(hits):
-        high, low = split(terms[...])
-        total = jnp.dot(hits[...], jnp.concatenate([high, low], axis=1), preferred_element_type=F32)
-        return total[:, 0:side] + total[:, side:]
+    def add_up(hits, part):
+        blocks = hits.shape[0]
+        for k in range(0, vecs, 2):
+            halves = [split(terms[pl.ds(k + m, slots, stride=vecs), :]) for m in range(2)]
+            stacked = jnp.concatenate([jnp.concatenate(half, axis=0) for half in halves], axis=1)
+            total = jnp.dot(hits, stacked, preferred_element_type=F32)
+            for m in range(2):
+                part[pl.ds(k + m, blocks, stride=vecs), :] = total[:, m * side:(m + 1) * side]
 
     def first(step, carry):
         for u in range(UNROLL):
@@ -132,12 +144,12 @@
                 terms[pl.ds(place + q * vecs, vecs), :] = own[0:vecs] + own[vecs:]
         return carry
 
-    lax.fori_loop(0, slots // (GROUP * UNROLL), first, 0)
-    row_part[...] = add_up(row_hits).reshape(row_blocks, vecs, side)
+    lax.fori_loop(0, steps, first, 0)
+    add_up(row_hits, row_part)
     rowp = []
     for n, peer in enumerate(col_peers):
         rowp.append(pltpu.make_async_remote_copy(
-            src_ref=row_part.at[pl.ds(peer[1] * local, local)], dst_ref=row_in.at[n],
+            src_ref=row_part.at[pl.ds(pl.multiple_of(peer[1] * span, span), span)], dst_ref=row_in.at[n],
             send_sem=rowp_send.at[n], recv_sem=rowp_recv.at[n], device_id=peer, device_id_type=MESH))
         rowp[-1].start()
 
@@ -170,16 +182,16 @@
                 terms[pl.ds(place + q * vecs, vecs), :] = own[:, 0:side] + own[:, side:]
         return carry
 
-    lax.fori_loop(0, slots // (GROUP * UNROLL), second, 0)
-    col_part[...] = add_up(col_hits).reshape(col_blocks, vecs, side)
+    lax.fori_loop(0, steps, second, 0)
+    add_up(col_hits, col_part)
     colp = []
     for n, peer in enumerate(row_peers):
         colp.append(pltpu.make_async_remote_copy(
-            src_ref=col_part.at[pl.ds(peer[0] * local, local)], dst_ref=col_in.at[n],
+            src_ref=col_part.at[pl.ds(pl.multiple_of(peer[0] * span, span), span)], dst_ref=col_in.at[n],
             send_sem=colp_send.at[n], recv_sem=colp_recv.at[n], device_id=peer, device_id_type=MESH))
         colp[-1].start()
 
-    total = row_part[pl.ds(c * local, local)] + col_part[pl.ds(r * local, local)]
+    total = row_part[pl.ds(pl.multiple_of(c * span, span), span)] + col_part[pl.ds(pl.multiple_of(r * span, span), span)]
     for n, copy in enumerate(rowp):
         copy.wait()
         total += row_in[n]
@@ -187,7 +199,7 @@
         copy.wait()
         total += col_in[n]
     for j in range(local):
-        out_ref[:, j * side:(j + 1) * side] = total[j]
+        out_ref[:, j * side:(j + 1) * side] = total[j * vecs:(j + 1) * vecs]
 
 
 def body(tiles, tile_rows, tile_cols, tile_counts, vectors):
@@ -219,13 +231,11 @@
             pltpu.VMEM((column_devices, vecs, width), F32),
             pltpu.VMEM((col_blocks, 2 * vecs, 2 * side), BF16),
             pltpu.VMEM((row_blocks, 2 * vecs, side), BF16),
-            pltpu.VMEM((row_blocks * vecs, slots * vecs), BF16),
-            pltpu.VMEM((col_blocks * vecs, slots * vecs), BF16),
             pltpu.VMEM((slots * vecs, side), F32),
-            pltpu.VMEM((row_blocks, vecs, side), F32),
-            pltpu.VMEM((col_blocks, vecs, side), F32),
-            pltpu.VMEM((column_devices - 1, local, vecs, side), F32),
-            pltpu.VMEM((row_devices - 1, local, vecs, side), F32),
+            pltpu.VMEM((row_blocks * vecs, side), F32),
+            pltpu.VMEM((col_blocks * vecs, side), F32),
+            pltpu.VMEM((column_devices - 1, local * vecs, side), F32),
+            pltpu.VMEM((row_devices - 1, local * vecs, side), F32),
             dma((7,)),
             dma((CHUNKS,)),
             dma((row_devices - 1,)),

time: 19.3 us -> 18.7 us (0.969)
  Pallas kernels: 17.9 us -> 17.2 us
    pallas_call x1, Pallas kernels: 17.9 us -> 17.2 us  [body(): pl.pallas_call(kernel, out_shape=pltpu.VMEM((vecs, width), F32), in_specs...]
where the time goes in v4:
time: 18.7 us; the launch traced here: 18.5 us
  Pallas kernels  17.2 us (92%)
  between operations  0.66 us (4%)
  local copies, waits for them, and re-layouts  0.61 us (3%)
    pallas_call x1, Pallas kernels, body(): pl.pallas_call(kernel, out_shape=pltpu.VMEM((vecs, width), F32), in_specs...  17.2 us
    unnamed x1, local copies, waits for them, and re-layouts  0.61 us

profile of v4, /device:TPU:0, one launch (start us, length us, event | category | flops | bytes accessed | tf_op | source)
XLA Modules:
  0.0 18.5 jit_solution(2021240504366671253)
XLA Ops:
  0.7 17.2 %symmetric_product.1 = f32[8,512]{1,0:T(8,128)S(1)} custom-call(s32[1,128]{1,0:T(1,128)} %bitcast.4, s32[1,128]{1,0:T(1,128)} %bitcast.5, s32[1,1]{1,0:T(1,128)S(6)} %copy.8.count_ref, f32[8,512]{1,0:T(8,128)} %x_ref.1, f32[128,128,128]{2,1,0:T(8,128)} %bitcast.3), custom_call_target="tpu_custom_call" | custom-call | flops 201326592 | bytes 8388608 | tf_op jit(solution)/shard_map/symmetric_product/pallas_call | solution.py:217
  17.9 0.6 %copy.7 = f32[8,512]{1,0:T(8,128)} copy(f32[8,512]{1,0:T(8,128)S(1)} %symmetric_product.1) | data formatting | bytes 32768

commit v5 on v4

--- a/solution.py
+++ b/solution.py
@@ -13,12 +13,18 @@
 CHUNKS = 8
 GROUP = 2
 UNROLL = 16
+AHEAD = 2
 
 
 def split(value):
     high = value.astype(BF16)
     low = (value - high.astype(F32)).astype(BF16)
     return high, low
+
+
+def stack(value):
+    high = value.astype(BF16).astype(F32)
+    return jnp.concatenate([high, value - high], axis=0).astype(BF16)
 
 
 def hit_matrix(labels, count, blocks):
@@ -31,7 +37,7 @@
 
 def kernel(
     rows_ref, cols_ref, count_ref, x_ref, tiles_ref, out_ref,
-    rows_s, cols_s, count_s, rows_v, cols_v, raw, both, col_x, row_x, col_lhs, row_lhs, terms, row_part, col_part, row_in, col_in,
+    rows_s, cols_s, count_s, rows_v, cols_v, raw, both, col_x, row_x, col_lhs, row_lhs, row_terms, col_terms, row_part, col_part, row_in, col_in,
     small_sem, tile_sem, colx_send, colx_recv, rowx_send, rowx_recv, rowp_send, rowp_recv, colp_send, colp_recv,
 ):
     row_devices = lax.axis_size("row")
@@ -91,7 +97,8 @@
         rowx[-1].start()
     for copy in smalls:
         copy.wait()
-    terms[...] = jnp.zeros_like(terms)
+    row_terms[...] = jnp.zeros_like(row_terms)
+    col_terms[...] = jnp.zeros_like(col_terms)
 
     def halve(n, carry):
         fetch(n).wait()
@@ -116,14 +123,12 @@
         copy.wait()
     for i in range(row_devices):
         for j in range(local):
-            high, low = split(col_x[i, :, j * side:(j + 1) * side])
             n = i * local + j
-            upper = jnp.concatenate([high, low], axis=0)
-            under = jnp.concatenate([high, jnp.zeros_like(low)], axis=0)
-            col_lhs[n, :, 0:side] = upper
-            col_lhs[n, :, side:] = under
-
-    def add_up(hits, part):
+            piece = stack(col_x[i, :, j * side:(j + 1) * side])
+            col_lhs[n, :, 0:side] = piece
+            col_lhs[n, :, side:] = piece
+
+    def add_up(hits, terms, part):
         blocks = hits.shape[0]
         for k in range(0, vecs, 2):
             halves = [split(terms[pl.ds(k + m, slots, stride=vecs), :]) for m in range(2)]
@@ -141,24 +146,30 @@
             place = pl.multiple_of(quad * GROUP * vecs, GROUP * vecs)
             for q in range(GROUP):
                 own = got[2 * q * vecs:2 * (q + 1) * vecs, q * side:(q + 1) * side]
-                terms[pl.ds(place + q * vecs, vecs), :] = own[0:vecs] + own[vecs:]
+                row_terms[pl.ds(place + q * vecs, vecs), :] = own[0:vecs] + own[vecs:]
         return carry
 
-    lax.fori_loop(0, steps, first, 0)
-    add_up(row_hits, row_part)
     rowp = []
     for n, peer in enumerate(col_peers):
         rowp.append(pltpu.make_async_remote_copy(
             src_ref=row_part.at[pl.ds(pl.multiple_of(peer[1] * span, span), span)], dst_ref=row_in.at[n],
             send_sem=rowp_send.at[n], recv_sem=rowp_recv.at[n], device_id=peer, device_id_type=MESH))
-        rowp[-1].start()
+
+    def finish_rows():
+        add_up(row_hits, row_terms, row_part)
+        for copy in rowp:
+            copy.start()
+
+    late = 2 * r >= row_devices
+    ahead = jnp.where(late, jnp.minimum(steps, AHEAD), steps)
+    lax.fori_loop(0, ahead, first, 0)
+    pl.when(jnp.logical_not(late))(finish_rows)
 
     for copy in rowx:
         copy.wait()
     for i in range(column_devices):
         for j in range(local):
-            high, low = split(row_x[i, :, j * side:(j + 1) * side])
-            row_lhs[i * local + j] = jnp.concatenate([high, low], axis=0)
+            row_lhs[i * local + j] = stack(row_x[i, :, j * side:(j + 1) * side])
 
     def second(step, carry):
         blank = jnp.zeros((2 * vecs, side), BF16)
@@ -179,17 +190,20 @@
                 h = q // 2
                 own = got[2 * q * vecs:2 * (q + 1) * vecs, 2 * h * side:2 * (h + 1) * side]
                 own = own[0:vecs] + own[vecs:]
-                terms[pl.ds(place + q * vecs, vecs), :] = own[:, 0:side] + own[:, side:]
+                col_terms[pl.ds(place + q * vecs, vecs), :] = own[:, 0:side] + own[:, side:]
         return carry
 
     lax.fori_loop(0, steps, second, 0)
-    add_up(col_hits, col_part)
+    add_up(col_hits, col_terms, col_part)
     colp = []
     for n, peer in enumerate(row_peers):
         colp.append(pltpu.make_async_remote_copy(
             src_ref=col_part.at[pl.ds(pl.multiple_of(peer[0] * span, span), span)], dst_ref=col_in.at[n],
             send_sem=colp_send.at[n], recv_sem=colp_recv.at[n], device_id=peer, device_id_type=MESH))
         colp[-1].start()
+
+    lax.fori_loop(ahead, steps, first, 0)
+    pl.when(late)(finish_rows)
 
     total = row_part[pl.ds(pl.multiple_of(c * span, span), span)] + col_part[pl.ds(pl.multiple_of(r * span, span), span)]
     for n, copy in enumerate(rowp):
@@ -232,6 +246,7 @@
             pltpu.VMEM((col_blocks, 2 * vecs, 2 * side), BF16),
             pltpu.VMEM((row_blocks, 2 * vecs, side), BF16),
             pltpu.VMEM((slots * vecs, side), F32),
+            pltpu.VMEM((slots * vecs, side), F32),
             pltpu.VMEM((row_blocks * vecs, side), F32),
             pltpu.VMEM((col_blocks * vecs, side), F32),
             pltpu.VMEM((column_devices - 1, local * vecs, side), F32),

time: 18.7 us -> 18.9 us (1.011)
  the two profiles are of different devices: /device:TPU:0 before, /device:TPU:2 now
where the time goes in v5:
time: 18.9 us; the launch traced here: 18.7 us
  Pallas kernels  17.5 us (93%)
  between operations  0.66 us (3%)
  local copies, waits for them, and re-layouts  0.61 us (3%)
    pallas_call x1, Pallas kernels, body(): pl.pallas_call(kernel, out_shape=pltpu.VMEM((vecs, width), F32), in_specs...  17.5 us
    unnamed x1, local copies, waits for them, and re-layouts  0.61 us

profile of v5, /device:TPU:2, one launch (start us, length us, event | category | flops | bytes accessed | tf_op | source)
XLA Modules:
  0.0 18.7 jit_solution(522950122802025539)
XLA Ops:
  0.7 17.5 %symmetric_product.1 = f32[8,512]{1,0:T(8,128)S(1)} custom-call(s32[1,128]{1,0:T(1,128)} %bitcast.4, s32[1,128]{1,0:T(1,128)} %bitcast.5, s32[1,1]{1,0:T(1,128)S(6)} %copy.8.count_ref, f32[8,512]{1,0:T(8,128)} %x_ref.1, f32[128,128,128]{2,1,0:T(8,128)} %bitcast.3), custom_call_target="tpu_custom_call" | custom-call | flops 201326592 | bytes 8388608 | tf_op jit(solution)/shard_map/symmetric_product/pallas_call | solution.py:231
  18.1 0.6 %copy.7 = f32[8,512]{1,0:T(8,128)} copy(f32[8,512]{1,0:T(8,128)S(1)} %symmetric_product.1) | data formatting | bytes 32768

commit v6 on v5

--- a/solution.py
+++ b/solution.py
@@ -13,7 +13,7 @@
 CHUNKS = 8
 GROUP = 2
 UNROLL = 16
-AHEAD = 2
+AHEAD = 1
 
 
 def split(value):
@@ -90,11 +90,16 @@
             src_ref=x_ref, dst_ref=col_x.at[r], send_sem=colx_send.at[n], recv_sem=colx_recv.at[n],
             device_id=peer, device_id_type=MESH))
         colx[-1].start()
-    for n, peer in enumerate(col_peers):
+    arrivals = []
+    for n in range(column_devices - 1):
+        other = jnp.where(n < c, n, n + 1)
         rowx.append(pltpu.make_async_remote_copy(
-            src_ref=x_ref, dst_ref=row_x.at[c], send_sem=rowx_send.at[n], recv_sem=rowx_recv.at[n],
-            device_id=peer, device_id_type=MESH))
+            src_ref=x_ref, dst_ref=row_x.at[c], send_sem=rowx_send.at[n], recv_sem=rowx_recv.at[c],
+            device_id=(r, other), device_id_type=MESH))
         rowx[-1].start()
+        arrivals.append(pltpu.make_async_remote_copy(
+            src_ref=x_ref, dst_ref=row_x.at[other], send_sem=rowx_send.at[n], recv_sem=rowx_recv.at[other],
+            device_id=(r, other), device_id_type=MESH))
     for copy in smalls:
         copy.wait()
     row_terms[...] = jnp.zeros_like(row_terms)
@@ -160,13 +165,14 @@
         for copy in rowp:
             copy.start()
 
-    late = 2 * r >= row_devices
+    late = jnp.logical_and(2 * r >= row_devices, c == 0)
     ahead = jnp.where(late, jnp.minimum(steps, AHEAD), steps)
     lax.fori_loop(0, ahead, first, 0)
     pl.when(jnp.logical_not(late))(finish_rows)
 
-    for copy in rowx:
-        copy.wait()
+    for sent, arrival in zip(rowx, arrivals):
+        sent.wait_send()
+        arrival.wait_recv()
     for i in range(column_devices):
         for j in range(local):
             row_lhs[i * local + j] = stack(row_x[i, :, j * side:(j + 1) * side])
@@ -256,7 +262,7 @@
             dma((row_devices - 1,)),
             dma((row_devices - 1,)),
             dma((column_devices - 1,)),
-            dma((column_devices - 1,)),
+            dma((column_devices,)),
             dma((column_devices - 1,)),
             dma((column_devices - 1,)),
             dma((row_devices - 1,)),

time: 18.9 us -> 17.3 us (0.915)
  the two profiles are of different devices: /device:TPU:2 before, /device:TPU:31 now
where the time goes in v6:
time: 17.3 us; the launch traced here: 17.2 us
  Pallas kernels  15.9 us (92%)
  between operations  0.66 us (4%)
  local copies, waits for them, and re-layouts  0.61 us (4%)
    pallas_call x1, Pallas kernels, body(): pl.pallas_call(kernel, out_shape=pltpu.VMEM((vecs, width), F32), in_specs...  15.9 us
    unnamed x1, local copies, waits for them, and re-layouts  0.61 us

profile of v6, /device:TPU:31, one launch (start us, length us, event | category | flops | bytes accessed | tf_op | source)
XLA Modules:
  0.0 17.2 jit_solution(7449977641807480331)
XLA Ops:
  0.7 15.9 %symmetric_product.1 = f32[8,512]{1,0:T(8,128)S(1)} custom-call(s32[1,128]{1,0:T(1,128)} %bitcast.4, s32[1,128]{1,0:T(1,128)} %bitcast.5, s32[1,1]{1,0:T(1,128)S(6)} %copy.8.count_ref, f32[8,512]{1,0:T(8,128)} %x_ref.1, f32[128,128,128]{2,1,0:T(8,128)} %bitcast.3), custom_call_target="tpu_custom_call" | custom-call | flops 201326592 | bytes 8388608 | tf_op jit(solution)/shard_map/symmetric_product/pallas_call | solution.py:237
  16.5 0.6 %copy.7 = f32[8,512]{1,0:T(8,128)} copy(f32[8,512]{1,0:T(8,128)S(1)} %symmetric_product.1) | data formatting | bytes 32768

commit v7 on v6

--- a/solution.py
+++ b/solution.py
@@ -10,7 +10,7 @@
 MESH = pl.DeviceIdType.MESH
 F32 = jnp.float32
 BF16 = jnp.bfloat16
-CHUNKS = 8
+CHUNKS = 4
 GROUP = 2
 UNROLL = 16
 AHEAD = 1
@@ -63,6 +63,34 @@
     for peer in row_peers + col_peers:
         pl.semaphore_signal(barrier, inc=1, device_id=peer, device_id_type=MESH)
 
+    def fetch(n):
+        piece = pl.ds(n * chunk, chunk)
+        return pltpu.make_async_copy(tiles_ref.at[piece], raw.at[piece], tile_sem.at[n])
+
+    def begin(n, carry):
+        fetch(n).start()
+        return carry
+
+    lax.fori_loop(0, chunks, begin, 0)
+    pl.semaphore_wait(barrier, len(row_peers) + len(col_peers))
+
+    colx, rowx, arrivals = [], [], []
+    for n, peer in enumerate(row_peers):
+        colx.append(pltpu.make_async_remote_copy(
+            src_ref=x_ref, dst_ref=col_x.at[r], send_sem=colx_send.at[n], recv_sem=colx_recv.at[n],
+            device_id=peer, device_id_type=MESH))
+    for n in range(column_devices - 1):
+        turn = 0 if n == 0 else lax.rem(c + column_devices - 2 + n, column_devices - 1) + 1
+        other = jnp.where(c == 0, n + 1, turn)
+        rowx.append(pltpu.make_async_remote_copy(
+            src_ref=x_ref, dst_ref=row_x.at[c], send_sem=rowx_send.at[n], recv_sem=rowx_recv.at[c],
+            device_id=(r, other), device_id_type=MESH))
+        arrivals.append(pltpu.make_async_remote_copy(
+            src_ref=x_ref, dst_ref=row_x.at[other], send_sem=rowx_send.at[n], recv_sem=rowx_recv.at[other],
+            device_id=(r, other), device_id_type=MESH))
+    for copy in rowx[:1] + colx + rowx[1:]:
+        copy.start()
+
     smalls = [
         pltpu.make_async_copy(source, target, small_sem.at[n])
         for n, (source, target) in enumerate([
@@ -72,34 +100,6 @@
     ]
     for copy in smalls:
         copy.start()
-
-    def fetch(n):
-        piece = pl.ds(n * chunk, chunk)
-        return pltpu.make_async_copy(tiles_ref.at[piece], raw.at[piece], tile_sem.at[n])
-
-    def begin(n, carry):
-        fetch(n).start()
-        return carry
-
-    lax.fori_loop(0, chunks, begin, 0)
-    pl.semaphore_wait(barrier, len(row_peers) + len(col_peers))
-
-    colx, rowx = [], []
-    for n, peer in enumerate(row_peers):
-        colx.append(pltpu.make_async_remote_copy(
-            src_ref=x_ref, dst_ref=col_x.at[r], send_sem=colx_send.at[n], recv_sem=colx_recv.at[n],
-            device_id=peer, device_id_type=MESH))
-        colx[-1].start()
-    arrivals = []
-    for n in range(column_devices - 1):
-        other = jnp.where(n < c, n, n + 1)
-        rowx.append(pltpu.make_async_remote_copy(
-            src_ref=x_ref, dst_ref=row_x.at[c], send_sem=rowx_send.at[n], recv_sem=rowx_recv.at[c],
-            device_id=(r, other), device_id_type=MESH))
-        rowx[-1].start()
-        arrivals.append(pltpu.make_async_remote_copy(
-            src_ref=x_ref, dst_ref=row_x.at[other], send_sem=rowx_send.at[n], recv_sem=rowx_recv.at[other],
-            device_id=(r, other), device_id_type=MESH))
     for copy in smalls:
         copy.wait()
     row_terms[...] = jnp.zeros_like(row_terms)

time: 17.3 us -> 17.2 us (level)
  no operation moved by 1% of the time
where the time goes in v7:
time: 17.2 us; the launch traced here: 17 us
  Pallas kernels  15.8 us (92%)
  between operations  0.66 us (4%)
  local copies, waits for them, and re-layouts  0.61 us (4%)
    pallas_call x1, Pallas kernels, body(): pl.pallas_call(kernel, out_shape=pltpu.VMEM((vecs, width), F32), in_specs...  15.8 us
    unnamed x1, local copies, waits for them, and re-layouts  0.61 us

profile of v7, /device:TPU:31, one launch (start us, length us, event | category | flops | bytes accessed | tf_op | source)
XLA Modules:
  0.0 17.0 jit_solution(11035219453192880085)
XLA Ops:
  0.7 15.8 %symmetric_product.1 = f32[8,512]{1,0:T(8,128)S(1)} custom-call(s32[1,128]{1,0:T(1,128)} %bitcast.4, s32[1,128]{1,0:T(1,128)} %bitcast.5, s32[1,1]{1,0:T(1,128)S(6)} %copy.8.count_ref, f32[8,512]{1,0:T(8,128)} %x_ref.1, f32[128,128,128]{2,1,0:T(8,128)} %bitcast.3), custom_call_target="tpu_custom_call" | custom-call | flops 201326592 | bytes 8388608 | tf_op jit(solution)/shard_map/symmetric_product/pallas_call | solution.py:237
  16.4 0.6 %copy.7 = f32[8,512]{1,0:T(8,128)} copy(f32[8,512]{1,0:T(8,128)S(1)} %symmetric_product.1) | data formatting | bytes 32768

commit v8 on v7

--- a/solution.py
+++ b/solution.py
@@ -72,6 +72,21 @@
         return carry
 
     lax.fori_loop(0, chunks, begin, 0)
+    def halve(n, carry):
+        fetch(n).wait()
+
+        def one(i, carry):
+            t = n * chunk + i
+            high, low = split(raw[t])
+            place = pl.ds(pl.multiple_of(t * side, side), side)
+            both[place, 0:side] = high
+            both[place, side:] = low
+            return carry
+
+        return lax.fori_loop(0, chunk, one, carry, unroll=8)
+
+    early = jnp.where(c == 0, chunks, 0)
+    lax.fori_loop(0, early, halve, 0)
     pl.semaphore_wait(barrier, len(row_peers) + len(col_peers))
 
     colx, rowx, arrivals = [], [], []
@@ -100,26 +115,13 @@
     ]
     for copy in smalls:
         copy.start()
-    for copy in smalls:
-        copy.wait()
     row_terms[...] = jnp.zeros_like(row_terms)
     col_terms[...] = jnp.zeros_like(col_terms)
 
-    def halve(n, carry):
-        fetch(n).wait()
-
-        def one(i, carry):
-            t = n * chunk + i
-            high, low = split(raw[t])
-            place = pl.ds(pl.multiple_of(t * side, side), side)
-            both[place, 0:side] = high
-            both[place, side:] = low
-            return carry
-
-        return lax.fori_loop(0, chunk, one, carry, unroll=8)
-
-    lax.fori_loop(0, chunks, halve, 0)
-
+    lax.fori_loop(early, chunks, halve, 0)
+
+    for copy in smalls:
+        copy.wait()
     count = count_s[0, 0]
     row_hits = hit_matrix(rows_v[...], count, row_blocks)
     col_hits = hit_matrix(cols_v[...], count, col_blocks)

time: 17.2 us -> 17.3 us (level)
  no operation moved by 1% of the time
where the time goes in v8:
time: 17.3 us; the launch traced here: 17.1 us
  Pallas kernels  15.8 us (91%)
  between operations  0.66 us (4%)
  local copies, waits for them, and re-layouts  0.61 us (4%)
    pallas_call x1, Pallas kernels, body(): pl.pallas_call(kernel, out_shape=pltpu.VMEM((vecs, width), F32), in_specs...  15.8 us
    unnamed x1, local copies, waits for them, and re-layouts  0.61 us

profile of v8, /device:TPU:31, one launch (start us, length us, event | category | flops | bytes accessed | tf_op | source)
XLA Modules:
  0.0 17.1 jit_solution(11363431150493775605)
XLA Ops:
  0.7 15.8 %symmetric_product.1 = f32[8,512]{1,0:T(8,128)S(1)} custom-call(s32[1,128]{1,0:T(1,128)} %bitcast.4, s32[1,128]{1,0:T(1,128)} %bitcast.5, s32[1,1]{1,0:T(1,128)S(6)} %copy.8.count_ref, f32[8,512]{1,0:T(8,128)} %x_ref.1, f32[128,128,128]{2,1,0:T(8,128)} %bitcast.3), custom_call_target="tpu_custom_call" | custom-call | flops 201326592 | bytes 8388608 | tf_op jit(solution)/shard_map/symmetric_product/pallas_call | solution.py:239
  16.4 0.6 %copy.7 = f32[8,512]{1,0:T(8,128)} copy(f32[8,512]{1,0:T(8,128)S(1)} %symmetric_product.1) | data formatting | bytes 32768

commit v9 on v8

--- a/solution.py
+++ b/solution.py
@@ -13,7 +13,7 @@
 CHUNKS = 4
 GROUP = 2
 UNROLL = 16
-AHEAD = 1
+AHEAD = 3
 
 
 def split(value):
@@ -72,6 +72,7 @@
         return carry
 
     lax.fori_loop(0, chunks, begin, 0)
+
     def halve(n, carry):
         fetch(n).wait()
 

time: 17.3 us -> 17.9 us (1.035)
  the two profiles are of different devices: /device:TPU:31 before, /device:TPU:0 now
where the time goes in v9:
time: 17.9 us; the launch traced here: 17.7 us
  Pallas kernels  16.4 us (92%)
  between operations  0.66 us (4%)
  local copies, waits for them, and re-layouts  0.61 us (3%)
    pallas_call x1, Pallas kernels, body(): pl.pallas_call(kernel, out_shape=pltpu.VMEM((vecs, width), F32), in_specs...  16.4 us
    unnamed x1, local copies, waits for them, and re-layouts  0.61 us

profile of v9, /device:TPU:0, one launch (start us, length us, event | category | flops | bytes accessed | tf_op | source)
XLA Modules:
  0.0 17.7 jit_solution(9134161649929367514)
XLA Ops:
  0.7 16.4 %symmetric_product.1 = f32[8,512]{1,0:T(8,128)S(1)} custom-call(s32[1,128]{1,0:T(1,128)} %bitcast.4, s32[1,128]{1,0:T(1,128)} %bitcast.5, s32[1,1]{1,0:T(1,128)S(6)} %copy.8.count_ref, f32[8,512]{1,0:T(8,128)} %x_ref.1, f32[128,128,128]{2,1,0:T(8,128)} %bitcast.3), custom_call_target="tpu_custom_call" | custom-call | flops 201326592 | bytes 8388608 | tf_op jit(solution)/shard_map/symmetric_product/pallas_call | solution.py:240
  17.0 0.6 %copy.7 = f32[8,512]{1,0:T(8,128)} copy(f32[8,512]{1,0:T(8,128)S(1)} %symmetric_product.1) | data formatting | bytes 32768
